TPU v7x, 32 devices: a whole 2x2x4 slice. The times are simulated.
32 devices in a mesh: narrow: 4 (over y, x), wide: 8 (over z, core).
Axes of the slice: x: 2, y: 2, z: 4, core: 2. Of those that a mesh axis runs over, the one named last changes fastest.
Arguments:
- tokens: bfloat16 [8, 2048, 768], P('wide', 'narrow'), may hold values from -6 to 6
- condition: bfloat16 [8, 2, 128], P('wide'), may hold values from -6 to 6
- docs_per_row: int32 [8], P('wide'), may hold values from 1 to 2, as said below
- w_ada: bfloat16 [128, 4608], replicated, may hold values from -0.5 to 0.5
- b_ada: bfloat16 [4608], replicated, may hold values from -3 to 3
- gain_one: bfloat16 [768], replicated, may hold values from 0.25 to 1.75
- w_qkv: bfloat16 [768, 2304], replicated, may hold values from -0.21875 to 0.21875
- w_out: bfloat16 [768, 768], replicated, may hold values from -1.75 to 1.75
- gain_two: bfloat16 [768], replicated, may hold values from 0.25 to 1.75
- w_up: bfloat16 [768, 3072], replicated, may hold values from -0.21875 to 0.21875
- b_up: bfloat16 [3072], replicated, may hold values from -3 to 3
- w_down: bfloat16 [3072, 768], replicated, may hold values from -0.109375 to 0.109375
- b_down: bfloat16 [768], replicated, may hold values from -3 to 3
- cotangent: bfloat16 [8, 2048, 768], P('wide', 'narrow'), may hold values from -6 to 6
Outputs:
- output: bfloat16 [8, 2048, 768], P('wide', 'narrow')
- grad_tokens: float32 [8, 2048, 768], P('wide', 'narrow')
- grad_condition: float32 [8, 2, 128], P('wide')
- grad_w_ada: float32 [128, 4608], P(None, 'wide')
- grad_b_ada: float32 [4608], P('wide')
- grad_gain_one: float32 [768], P('wide')
- grad_w_qkv: float32 [768, 2304], P('wide')
- grad_w_out: float32 [768, 768], P('wide')
- grad_gain_two: float32 [768], P('wide')
- grad_w_up: float32 [768, 3072], P('wide')
- grad_b_up: float32 [3072], P('wide')
- grad_w_down: float32 [3072, 768], P('wide')
- grad_b_down: float32 [768], P('wide')
Inputs may be any that keep to these rules, and one draw needn't show every extreme that they name: `docs_per_row`: each entry is 1 (the row is one sequence of 2048 tokens) or 2 (the row holds 2 sequences of 1024 tokens). In every draw the rows of some index of wide are all of the first kind and those of another index all of the second.
All inputs are finite; a program needn't handle non-finite values.
Results may differ from a plain program's by a relative error of at most 0.014.
The roundings to bfloat16 on the way count: a program that leaves them out, or rounds other values in their place, can miss the bound.
Values may be sent and summed in bfloat16 or wider, within the bound.
A program may use at most 192 MiB of HBM per device.

v0:
```python
import jax
import jax.numpy as jnp
from jax import lax
from jax.sharding import PartitionSpec as P

HEADS = 12
HEAD_DIM = 64
DOCS = 2
EPS = 1e-05
HIGH = lax.Precision.HIGHEST


def normalize(values):
    mean = jnp.mean(values, axis=-1, keepdims=True)
    centred = values - mean
    spread = jnp.mean(centred * centred, axis=-1, keepdims=True)
    return centred * lax.rsqrt(spread + EPS)


def modulated(values, gain, shift, scale):
    return normalize(values) * gain * (1.0 + scale) + shift


def gelu_tanh(values):
    return (
        0.5
        * values
        * (1.0 + jnp.tanh(0.7978845608028654 * (values + 0.044715 * values * values * values)))
    )


def rotate(values, cosine, sine):
    half = values.shape[-1] // 2
    turned = jnp.concatenate([-values[..., half:], values[..., :half]], axis=-1)
    return values * cosine + turned * sine


def angles(position, head_dim):
    freq = 10000.0 ** (-jnp.arange(head_dim // 2, dtype=jnp.float32) * 2.0 / head_dim)
    angle = position.astype(jnp.float32)[..., None] * freq
    angle = jnp.concatenate([angle, angle], axis=-1)
    return (jnp.cos(angle), jnp.sin(angle))


def attend(query, keys, values, docs):
    length, group, head_dim = query.shape
    count = length // docs
    block = min(512, count)
    factor = head_dim ** (-0.5)
    keys_doc = keys.reshape(count, docs, group, head_dim)
    values_doc = values.reshape(count, docs, group, head_dim)
    pieces = query.reshape(count // block, block, docs, group, head_dim)

    def one_block(piece):
        scores = (
            jnp.einsum("qshd,kshd->shqk", piece, keys_doc, preferred_element_type=jnp.float32)
            * factor
        )
        top = jnp.max(scores, axis=-1, keepdims=True)
        weights = jnp.exp(scores - top)
        total = jnp.sum(weights, axis=-1, keepdims=True)
        probs = (weights / total).astype(jnp.bfloat16)
        mixed = jnp.einsum("shqk,kshd->qshd", probs, values_doc, preferred_element_type=jnp.float32)
        return (mixed.astype(jnp.bfloat16), (top + jnp.log(total))[..., 0])

    mixed, logsum = lax.map(one_block, pieces)
    logsum = jnp.transpose(logsum, (0, 3, 1, 2)).reshape(length, group)
    return (mixed.reshape(length, group, head_dim), logsum)


def attend_back(query, keys, values, logsum, grad_out, docs):
    length, group, head_dim = query.shape
    count = length // docs
    block = min(512, count)
    factor = head_dim ** (-0.5)
    keys_doc = keys.reshape(count, docs, group, head_dim)
    values_doc = values.reshape(count, docs, group, head_dim)
    pieces = query.reshape(count // block, block, docs, group, head_dim)
    sum_pieces = logsum.reshape(count // block, block, docs, group)
    grad_pieces = grad_out.reshape(count // block, block, docs, group, head_dim)

    def step(carry, item):
        grad_keys, grad_values = carry
        piece, sum_piece, grad_piece = item
        scores = (
            jnp.einsum("qshd,kshd->shqk", piece, keys_doc, preferred_element_type=jnp.float32)
            * factor
        )
        probs = jnp.exp(scores - jnp.transpose(sum_piece, (1, 2, 0))[..., None])
        low_probs = probs.astype(jnp.bfloat16)
        grad_values = grad_values + jnp.einsum(
            "shqk,qshd->kshd", low_probs, grad_piece, preferred_element_type=jnp.float32
        )
        grad_probs = jnp.einsum(
            "qshd,kshd->shqk", grad_piece, values_doc, preferred_element_type=jnp.float32
        )
        centre = jnp.sum(grad_probs * probs, axis=-1, keepdims=True)
        grad_scores = (probs * (grad_probs - centre)).astype(jnp.bfloat16)
        grad_query = (
            jnp.einsum("shqk,kshd->qshd", grad_scores, keys_doc, preferred_element_type=jnp.float32)
            * factor
        )
        grad_keys = (
            grad_keys
            + jnp.einsum("shqk,qshd->kshd", grad_scores, piece, preferred_element_type=jnp.float32)
            * factor
        )
        return ((grad_keys, grad_values), grad_query)

    zeros = jnp.zeros((count, docs, group, head_dim), jnp.float32)
    (grad_keys, grad_values), grad_query = lax.scan(
        step, (zeros, zeros), (pieces, sum_pieces, grad_pieces)
    )
    shape = (length, group, head_dim)
    return (
        grad_query.reshape(shape).astype(jnp.bfloat16),
        grad_keys.reshape(shape).astype(jnp.bfloat16),
        grad_values.reshape(shape).astype(jnp.bfloat16),
    )


def attend_row(item):
    query, keys, values, docs = item
    return lax.cond(
        docs == 1, lambda: attend(query, keys, values, 1), lambda: attend(query, keys, values, DOCS)
    )


def back_row(item):
    query, keys, values, logsum, grad_out, docs = item
    return lax.cond(
        docs == 1,
        lambda: attend_back(query, keys, values, logsum, grad_out, 1),
        lambda: attend_back(query, keys, values, logsum, grad_out, DOCS),
    )


def body(
    tokens,
    condition,
    docs_per_row,
    w_ada,
    b_ada,
    gain_one,
    w_qkv,
    w_out,
    gain_two,
    w_up,
    b_up,
    w_down,
    b_down,
    cotangent,
):
    count_rows, local, width = tokens.shape
    shards = lax.axis_size("narrow")
    group = HEADS // shards
    head_dim = HEAD_DIM
    length = local * shards
    index = lax.axis_index("narrow") * local + jnp.arange(local, dtype=jnp.int32)
    kinds = docs_per_row[:, None]
    segment = index[None, :] % kinds
    position = index[None, :] // kinds
    cosine, sine = angles(position, head_dim)
    cosine = cosine[:, :, None, :]
    sine = sine[:, :, None, :]
    onehot = (segment[:, :, None] == jnp.arange(DOCS, dtype=jnp.int32)).astype(jnp.float32)
    mods = jnp.einsum(
        "rsc,cm->rsm", condition, w_ada, preferred_element_type=jnp.float32
    ) + b_ada.astype(jnp.float32)
    per_token = jnp.einsum("rls,rsm->rlm", onehot, mods, precision=HIGH)
    shift_one, scale_one, gate_one, shift_two, scale_two, gate_two = jnp.split(
        per_token, 6, axis=-1
    )
    inputs = tokens.astype(jnp.float32)
    first_in, first_back = jax.vjp(
        modulated, inputs, gain_one.astype(jnp.float32), shift_one, scale_one
    )
    first_low = first_in.astype(jnp.bfloat16).reshape(-1, width)
    projected = jnp.dot(first_low, w_qkv, preferred_element_type=jnp.float32).reshape(
        count_rows, local, 3, HEADS, head_dim
    )
    query_rot, turn_back = jax.vjp(lambda values: rotate(values, cosine, sine), projected[:, :, 0])
    key_rot = rotate(projected[:, :, 1], cosine, sine)

    def to_heads(values):
        return values.astype(jnp.bfloat16).reshape(count_rows, local, shards, group * head_dim)

    def head_view(values):
        return values.reshape(count_rows, length, group, head_dim)

    query_h, key_h, value_h = (
        lax.all_to_all(to_heads(query_rot), "narrow", split_axis=2, concat_axis=1, tiled=True),
        lax.all_to_all(to_heads(key_rot), "narrow", split_axis=2, concat_axis=1, tiled=True),
        lax.all_to_all(
            to_heads(projected[:, :, 2]), "narrow", split_axis=2, concat_axis=1, tiled=True
        ),
    )
    query_h = head_view(query_h)
    key_h = head_view(key_h)
    value_h = head_view(value_h)
    mixed_h, logsum = lax.map(attend_row, (query_h, key_h, value_h, docs_per_row))
    mixed = lax.all_to_all(
        mixed_h.reshape(count_rows, length, 1, group * head_dim),
        "narrow",
        split_axis=1,
        concat_axis=2,
        tiled=True,
    )
    attended = mixed.reshape(count_rows * local, width)
    branch = jnp.dot(attended, w_out, preferred_element_type=jnp.float32).reshape(
        count_rows, local, width
    )
    middle = inputs + gate_one * branch
    second_in, second_back = jax.vjp(
        modulated, middle, gain_two.astype(jnp.float32), shift_two, scale_two
    )
    second_low = second_in.astype(jnp.bfloat16).reshape(-1, width)
    hidden = jnp.dot(second_low, w_up, preferred_element_type=jnp.float32) + b_up.astype(
        jnp.float32
    )
    active, active_back = jax.vjp(gelu_tanh, hidden)
    active_low = active.astype(jnp.bfloat16)
    down = (
        jnp.dot(active_low, w_down, preferred_element_type=jnp.float32) + b_down.astype(jnp.float32)
    ).reshape(count_rows, local, width)
    output = (middle + gate_two * down).astype(jnp.bfloat16)
    grad_y = cotangent.astype(jnp.float32)
    grad_gate_two = grad_y * down
    grad_down = (grad_y * gate_two).astype(jnp.bfloat16).reshape(-1, width)
    sum_b_down = jnp.sum(grad_down.astype(jnp.float32), axis=0)
    sum_w_down = jnp.einsum("tf,td->fd", active_low, grad_down, preferred_element_type=jnp.float32)
    grad_active = jnp.einsum("td,fd->tf", grad_down, w_down, preferred_element_type=jnp.float32)
    grad_hidden = active_back(grad_active)[0].astype(jnp.bfloat16)
    sum_b_up = jnp.sum(grad_hidden.astype(jnp.float32), axis=0)
    sum_w_up = jnp.einsum("td,tf->df", second_low, grad_hidden, preferred_element_type=jnp.float32)
    grad_second = jnp.einsum(
        "tf,df->td", grad_hidden, w_up, preferred_element_type=jnp.float32
    ).reshape(count_rows, local, width)
    grad_middle_norm, sum_gain_two, grad_shift_two, grad_scale_two = second_back(grad_second)
    grad_middle = grad_y + grad_middle_norm
    grad_gate_one = grad_middle * branch
    grad_branch = (grad_middle * gate_one).astype(jnp.bfloat16).reshape(-1, width)
    sum_w_out = jnp.einsum("td,te->de", attended, grad_branch, preferred_element_type=jnp.float32)
    grad_attended = jnp.einsum(
        "te,de->td", grad_branch, w_out, preferred_element_type=jnp.float32
    ).astype(jnp.bfloat16)
    grad_mixed = lax.all_to_all(
        grad_attended.reshape(count_rows, local, shards, group * head_dim),
        "narrow",
        split_axis=2,
        concat_axis=1,
        tiled=True,
    )
    grad_mixed = head_view(grad_mixed)
    grad_query_h, grad_key_h, grad_value_h = lax.map(
        back_row, (query_h, key_h, value_h, logsum, grad_mixed, docs_per_row)
    )

    def from_heads(values):
        return values.reshape(count_rows, length, 1, group * head_dim)

    grad_query, grad_key, grad_value = (
        lax.all_to_all(from_heads(grad_query_h), "narrow", split_axis=1, concat_axis=2, tiled=True),
        lax.all_to_all(from_heads(grad_key_h), "narrow", split_axis=1, concat_axis=2, tiled=True),
        lax.all_to_all(from_heads(grad_value_h), "narrow", split_axis=1, concat_axis=2, tiled=True),
    )
    seq_shape = (count_rows, local, HEADS, head_dim)
    grad_query_raw = turn_back(grad_query.reshape(seq_shape).astype(jnp.float32))[0]
    grad_key_raw = turn_back(grad_key.reshape(seq_shape).astype(jnp.float32))[0]
    grad_projected = jnp.stack(
        [grad_query_raw, grad_key_raw, grad_value.reshape(seq_shape).astype(jnp.float32)], axis=2
    )
    grad_projected = grad_projected.astype(jnp.bfloat16).reshape(-1, 3 * width)
    sum_w_qkv = jnp.einsum(
        "td,te->de", first_low, grad_projected, preferred_element_type=jnp.float32
    )
    grad_first = jnp.einsum(
        "te,de->td", grad_projected, w_qkv, preferred_element_type=jnp.float32
    ).reshape(count_rows, local, width)
    grad_inputs_norm, sum_gain_one, grad_shift_one, grad_scale_one = first_back(grad_first)
    grad_inputs = grad_middle + grad_inputs_norm
    grad_per = jnp.concatenate(
        [
            grad_shift_one,
            grad_scale_one,
            grad_gate_one,
            grad_shift_two,
            grad_scale_two,
            grad_gate_two,
        ],
        axis=-1,
    )
    grad_mods = jnp.einsum("rls,rlm->rsm", onehot, grad_per, precision=HIGH)
    sum_b_ada = jnp.sum(grad_mods, axis=(0, 1))
    sum_w_ada_turned = jnp.einsum(
        "rsm,rsc->mc", grad_mods, condition.astype(jnp.float32), precision=HIGH
    )
    grad_cond_part = jnp.einsum("rsm,cm->rsc", grad_mods, w_ada.astype(jnp.float32), precision=HIGH)
    (
        share_ada,
        share_qkv,
        share_out,
        share_up,
        share_down,
        piece_ada,
        piece_one,
        piece_two,
        piece_up,
        piece_down,
    ) = (
        lax.psum_scatter(sum_w_ada_turned, "wide", scatter_dimension=0, tiled=True),
        lax.psum_scatter(sum_w_qkv, "wide", scatter_dimension=0, tiled=True),
        lax.psum_scatter(sum_w_out, "wide", scatter_dimension=0, tiled=True),
        lax.psum_scatter(sum_w_up, "wide", scatter_dimension=0, tiled=True),
        lax.psum_scatter(sum_w_down, "wide", scatter_dimension=0, tiled=True),
        lax.psum_scatter(sum_b_ada, "wide", scatter_dimension=0, tiled=True),
        lax.psum_scatter(sum_gain_one, "wide", scatter_dimension=0, tiled=True),
        lax.psum_scatter(sum_gain_two, "wide", scatter_dimension=0, tiled=True),
        lax.psum_scatter(sum_b_up, "wide", scatter_dimension=0, tiled=True),
        lax.psum_scatter(sum_b_down, "wide", scatter_dimension=0, tiled=True),
    )
    (
        total_ada,
        total_qkv,
        total_out,
        total_up,
        total_down,
        vector_ada,
        vector_one,
        vector_two,
        vector_up,
        vector_down,
        grad_condition,
    ) = lax.psum(
        (
            share_ada,
            share_qkv,
            share_out,
            share_up,
            share_down,
            piece_ada,
            piece_one,
            piece_two,
            piece_up,
            piece_down,
            grad_cond_part,
        ),
        "narrow",
    )
    return (
        output,
        grad_inputs,
        grad_condition,
        total_ada.T,
        vector_ada,
        vector_one,
        total_qkv,
        total_out,
        vector_two,
        total_up,
        vector_up,
        total_down,
        vector_down,
    )


def solution(mesh):
    in_specs = (
        P("wide", "narrow", None),
        P("wide", None, None),
        P("wide"),
        P(),
        P(),
        P(),
        P(),
        P(),
        P(),
        P(),
        P(),
        P(),
        P(),
        P("wide", "narrow", None),
    )
    out_specs = (
        P("wide", "narrow", None),
        P("wide", "narrow", None),
        P("wide", None, None),
        P(None, "wide"),
        P("wide"),
        P("wide"),
        P("wide", None),
        P("wide", None),
        P("wide"),
        P("wide", None),
        P("wide"),
        P("wide", None),
        P("wide"),
    )
    return jax.shard_map(body, mesh=mesh, in_specs=in_specs, out_specs=out_specs, check_vma=False)
```

profile of v0, /device:TPU:0, one launch (start us, length us, event | category | flops | bytes accessed | tf_op | source)
XLA Modules:
  0.0 913.8 jit_solution(2107163655373730929)
XLA Ops:
  12.2 5.9 copy.309
  23.5 4.2 copy-done.38
  32.1 5.2 all-to-all-start.2
  43.5 4.6 all-to-all-done.2
  48.1 13.2 %all_to_all.102 = bf16[1,512,4,192]{1,3,0,2:T(8,128)(2,1)S(1)} all-to-all(bf16[1,512,4,192]{1,3,0,2:T(8,128)(2,1)S(1)} %get-tuple-element.723), channel_id=1, replica_groups=mesh['narrow'=4,'wide'=8] {'narrow'}, dimensions={2} | all-to-all | bytes 1572864 | tf_op jit(solution)/shard_map/all_to_all | solution.py:193
  78.2 46.7 %conditional.2 = (bf16[2048,3,64]{2,1,0:T(4,128)(2,1)}, f32[2048,3]{1,0:T(8,128)}) conditional(s32[]{:T(128)} %convert_element_type.263, (bf16[2048,3,64]{0,2,1:T(8,128)(2,1)}, bf16[2048,3,64]{0,2,1:T(8,128)(2,1)S(1)}, bf16[2048,3,64]{0,2,1:T(8,128)(2,1)S(1)}) %tuple.47, (bf16[2048,3,64]{0,2,1:T(8,128)(2,1)}, bf16[2048,3,64]{0,2,1:T(8,128)(2,1)S(1)}, ...), branch_computations={%region_2.7_spmd, %region_7.12_spmd} | conditional | flops 833811456 | bytes 60920124 | solution.py:124
  82.7 36.1 %while.50 = (s32[]{:T(128)}, bf16[4,512,1,3,64]{1,4,3,2,0:T(8,128)(2,1)}, f32[4,1,3,512]{3,2,1,0:T(4,128)}, bf16[4,512,1,3,64]{1,4,3,2,0:T(8,128)(2,1)S(1)}, bf1...) while((s32[]{:T(128)}, bf16[4,512,1,3,64]{1,4,3,2,0:T(8,128)(2,1)}, ...), condition=%wide.region_11.11_spmd, body=%wide.region_8.10_spmd.sunk | while | flops 833714688 | bytes 39766112 | solution.py:66
  132.0 13.6 %reduce.17 = bf16[2048,192]{1,0:T(8,128)(2,1)} reduce(bf16[2048,1,1,192]{3,2,1,0:T(2,128)(2,1)} %bitcast.455, bf16[]{:T(256)} %broadcast.557), dimensions={1,2}, to_apply=%bitcast.292.reduce_sub_computation | reduce | bytes 1572866
  149.6 4.7 all-to-all-start.3
  158.7 4.1 all-to-all-done.3
  162.8 4.2 reshape.987
  166.9 5.7 copy.321
  186.6 11.7 %convert_reduce_fusion = (f32[3072]{0:T(1024)}, bf16[512,3072]{1,0:T(8,128)(2,1)S(1)}) fusion(f32[512,3072]{1,0:T(8,128)S(1)} %fusion.152, f32[3072]{0:T(1024)S(1)} %copy-done.87, bf16[512,768]{1,0:T(8,128)(2,1)S(1)} %copy-done.53, bf16[3072,768]{1,0:T(8,128)(2,1)} %param.37), kind=kOutput, calls=%fused_computation.105 | convolution fusion | flops 2458383360 | bytes 14966784 | tf_op jit(solution)/shard_map/td,fd->tf/dot_general | solution.py:232
  202.1 8.5 fusion.146
  215.8 11.2 %all_to_all.103 = bf16[1,512,4,192]{1,3,0,2:T(8,128)(2,1)S(1)} all-to-all(bf16[1,512,4,192]{1,3,0,2:T(8,128)(2,1)S(1)} %bitcast.488), channel_id=1, replica_groups=mesh['narrow'=4,'wide'=8] {'narrow'}, dimensions={2} | all-to-all | bytes 1572864 | tf_op jit(solution)/shard_map/all_to_all | solution.py:247
  229.1 117.1 %conditional.3 = (bf16[2048,3,64]{2,1,0:T(4,128)(2,1)}, bf16[2048,3,64]{2,1,0:T(4,128)(2,1)}, bf16[2048,3,64]{2,1,0:T(4,128)(2,1)S(1)}) conditional(s32[]{:T(128)} %convert_element_type.263, (bf16[2048,3,64]{0,2,1:T(8,128)(2,1)}, f32[2048,3]{1,0:T(8,128)S(1)}, bf16[2048,3,64]{0,2,1:T(8,128)(2,1)}, bf16[2048,3,64]{0,2,1:T(8,128)(2,1)S(1)}, ...), branch_computations={%region_16.20_spmd, %region_20.24_spmd} | conditional | flops 2053174272 | bytes 155857408 | solution.py:131
  239.2 96.6 %while.53 = (s32[]{:T(128)}, f32[2048,1,3,64]{0,3,2,1:T(8,128)}, f32[2048,1,3,64]{0,3,2,1:T(8,128)}, bf16[4,512,1,3,64]{1,4,3,2,0:T(8,128)(2,1)}, bf16[4,512,1,3...) while((s32[]{:T(128)}, f32[2048,1,3,64]{0,3,2,1:T(8,128)}, ...), condition=%wide.region_23.23_spmd.clone, body=%wide.region_21.22_spmd.clone.sunk | while | flops 2053077504 | bytes 129415344 | solution.py:111
  248.4 4.7 multiply_convert_fusion.8
  253.1 5.6 fusion.230
  263.1 5.1 fusion.229
  271.8 4.7 multiply_convert_fusion.8
  276.5 5.6 fusion.230
  287.9 5.1 fusion.229
  296.6 4.7 multiply_convert_fusion.8
  301.3 5.6 fusion.230
  312.7 5.1 fusion.229
  321.5 4.7 multiply_convert_fusion.8
  326.2 5.6 fusion.230
  335.7 4.2 copy.306
  352.9 12.7 %reduce.20 = bf16[2048,192]{1,0:T(8,128)(2,1)S(1)} reduce(bf16[2048,1,1,192]{3,2,1,0:T(2,128)(2,1)} %bitcast.458, bf16[]{:T(256)} %broadcast.557), dimensions={1,2}, to_apply=%bitcast.296.reduce_sub_computation | reduce | bytes 1572866
  367.9 4.2 all-to-all-start.6
  378.7 13.6 %reduce.19 = bf16[2048,192]{1,0:T(8,128)(2,1)} reduce(bf16[2048,1,1,192]{3,2,1,0:T(2,128)(2,1)} %bitcast.459, bf16[]{:T(256)} %broadcast.557), dimensions={1,2}, to_apply=%bitcast.298.reduce_sub_computation | reduce | bytes 1572866
  396.4 4.2 all-to-all-start.5
  407.0 11.6 %reduce.18 = bf16[2048,192]{1,0:T(8,128)(2,1)S(1)} reduce(bf16[2048,1,1,192]{3,2,1,0:T(2,128)(2,1)S(1)} %bitcast.456, bf16[]{:T(256)} %broadcast.557), dimensions={1,2}, to_apply=%bitcast.294.reduce_sub_computation | reduce | bytes 1572866
  429.3 4.1 all-to-all-start.7
  433.5 4.2 reshape.993
  437.7 4.5 copy.334
  452.1 4.9 copy.342
  481.3 5.0 fusion.120
  487.4 10.4 %fusion.142 = f32[3072,768]{1,0:T(8,128)} fusion(bf16[512,768]{1,0:T(8,128)(2,1)S(1)} %copy-done.54, f32[512,3072]{1,0:T(8,128)} %copy-done.28, f32[3072]{0:T(1024)S(1)} %copy-done.88), kind=kOutput, calls=%fused_computation.224 | convolution fusion | flops 2431647744 | bytes 16527360 | tf_op jit(solution)/shard_map/tf,td->fd/dot_general | solution.py:231
  499.0 7.0 fusion.154
  506.2 13.5 %reduce-scatter.6.cloned.1.call-done = f32[576,128]{1,0:T(8,128)} async-done(((f32[4608,128]{1,0:T(8,128)}), f32[576,128]{1,0:T(8,128)}) %reduce-scatter.6.cloned.1.call-update) | async-done | bytes 294928 | tf_op jit(solution)/shard_map/reduce_scatter | solution.py:311
  519.6 78.7 %reduce-scatter.8.cloned.1.call-done = f32[96,2304]{1,0:T(8,128)} async-done(((f32[768,2304]{1,0:T(8,128)}), f32[96,2304]{1,0:T(8,128)}) %reduce-scatter.8.cloned.1.call-update) | async-done | bytes 884752 | tf_op jit(solution)/shard_map/reduce_scatter | solution.py:312
  598.3 100.1 %reduce-scatter.14.cloned.1.call-done = f32[384,768]{1,0:T(8,128)} async-done(((f32[3072,768]{1,0:T(8,128)}), f32[384,768]{1,0:T(8,128)}) %reduce-scatter.14.cloned.1.call-update) | async-done | bytes 1179664 | tf_op jit(solution)/shard_map/reduce_scatter | solution.py:315
  698.4 100.0 %reduce-scatter.12.cloned.1.call-done = f32[96,3072]{1,0:T(8,128)} async-done(((f32[768,3072]{1,0:T(8,128)}), f32[96,3072]{1,0:T(8,128)}) %reduce-scatter.12.cloned.1.call-update) | async-done | bytes 1179664 | tf_op jit(solution)/shard_map/reduce_scatter | solution.py:314
  801.1 26.4 %all-reduce.9 = (f32[4608]{0:T(1024)S(1)}, f32[768]{0:T(1024)S(1)}, f32[768]{0:T(1024)S(1)}, f32[3072]{0:T(1024)S(1)}, f32[768]{0:T(1024)S(1)}) all-reduce(f32[4608]{0:T(1024)S(1)} %copy-done.65, f32[768]{0:T(1024)S(1)} %get-tuple-element.622, f32[768]{0:T(1024)S(1)} %copy-done.91, ...), channel_id=3, replica_groups=mesh['narrow'=4,'wide'=8] {'wide'}, use_global_device_ids=true, to_apply=%region_30.31.clone | all-reduce | flops 9984 | bytes 79872
  828.9 10.9 %all-reduce.10 = (f32[1,2,128]{2,1,0:T(2,128)}, f32[576]{0:T(1024)}, f32[96]{0:T(128)}, f32[96]{0:T(128)}, f32[384]{0:T(512)}, /*index=5*/f32[96]{0:T(128)}) all-reduce(f32[1,2,128]{2,1,0:T(2,128)S(1)} %convolution_bitcast_fusion.2, f32[576]{0:T(1024)S(1)} %dynamic-slice.2, ...), channel_id=1, replica_groups=mesh['narrow'=4,'wide'=8] {'narrow'}, use_global_device_ids=true, to_apply=%region_26.27 | all-reduce | flops 1504 | bytes 12032 | tf_op jit(solution)/shard_map/psum | solution.py:334
  839.7 60.2 %all-reduce.14.cloned.1.call-done = (f32[128,576]{0,1:T(8,128)}, f32[96,2304]{1,0:T(8,128)}, f32[96,768]{1,0:T(8,128)}, f32[96,3072]{1,0:T(8,128)}, f32[384,768]{1,0:T(8,128)}) async-done(((f32[128,576]{0,1:T(8,128)}, f32[96,2304]{1,0:T(8,128)}, f32[96,768]{1,0:T(8,128)}, f32[96,3072]{1,0:T(8,128)}, f32[384,768]{1,0:T(8,128)}), (f32[128,576]{0,1:T(8,128)}, f32[96,2304]{1,0:T(8,128)}, f32[96,768]{1,0:T(8,128)}, ...) | async-done | bytes 3833872 | tf_op jit(solution)/shard_map/psum | solution.py:334
  (350 shorter events, 260.7 us)
Async XLA Ops:
  7.2 170.0 %copy-start = (bf16[768,768]{1,0:T(8,128)(2,1)S(1)}, bf16[768,768]{1,0:T(8,128)(2,1)}, u32[]{:S(2)}) copy-start(bf16[768,768]{1,0:T(8,128)(2,1)} %param.33) | copy-start | bytes 3538948
  9.3 13.7 %copy-start.68 = (f32[512]{0:T(512)}, f32[512]{0:T(512)S(1)}, u32[]{:S(2)}) copy-start(f32[512]{0:T(512)S(1)} %broadcast_multiply_fusion.4) | copy-start | bytes 6148
  10.8 12.2 %copy-start.70 = (f32[512]{0:T(512)}, f32[512]{0:T(512)S(1)}, u32[]{:S(2)}) copy-start(f32[512]{0:T(512)S(1)} %fusion.136) | copy-start | bytes 6148
  11.5 11.5 %copy-start.63 = (f32[768]{0:T(1024)}, f32[768]{0:T(1024)S(1)}, u32[]{:S(2)}) copy-start(f32[768]{0:T(1024)S(1)} %convert_element_type.264) | copy-start | bytes 9220
  12.2 5.9 copy-start.35
  12.2 5.9 copy-start.93
  23.0 6.7 copy-start.6
  23.5 6.2 copy-start.40
  32.1 16.0 %all-to-all-start.2 = ((bf16[1,512,4,192]{1,3,0,2:T(8,128)(2,1)}), bf16[1,512,4,192]{1,3,0,2:T(8,128)(2,1)S(1)}, u32[]{:S(2)}, u32[]{:S(2)}) async-start(bf16[1,512,4,192]{1,3,0,2:T(8,128)(2,1)} %bitcast.65), calls=%async_computation.2 | async-start | bytes 1572864 | tf_op jit(solution)/shard_map/all_to_all | solution.py:194
  61.3 12.6 %all-to-all-start = ((bf16[1,512,4,192]{1,3,0,2:T(8,128)(2,1)}), bf16[1,512,4,192]{1,3,0,2:T(8,128)(2,1)S(1)}, u32[]{:S(2)}, u32[]{:S(2)}) async-start(bf16[1,512,4,192]{1,3,0,2:T(8,128)(2,1)} %get-tuple-element.724), calls=%async_computation | async-start | bytes 1572864 | tf_op jit(solution)/shard_map/all_to_all | solution.py:192
  145.6 8.7 copy-start.92
  145.6 9.4 %copy-start.90 = (bf16[3072]{0:T(1024)(128)(2,1)S(1)}, bf16[3072]{0:T(1024)(128)(2,1)}, u32[]{:S(2)}) copy-start(bf16[3072]{0:T(1024)(128)(2,1)} %param.36) | copy-start | bytes 18436
  145.6 10.0 %copy-start.18 = (bf16[1,512,768]{2,1,0:T(8,128)(2,1)S(1)}, bf16[1,512,768]{2,1,0:T(8,128)(2,1)}, u32[]{:S(2)}) copy-start(bf16[1,512,768]{2,1,0:T(8,128)(2,1)} %param.39) | copy-start | bytes 2359300
  149.6 13.1 %all-to-all-start.3 = ((bf16[4,2,49152]{2,1,0:T(2,128)(2,1)}), bf16[4,2,49152]{2,1,0:T(2,128)(2,1)}, u32[]{:S(2)}, u32[]{:S(2)}) async-start(bf16[4,2,49152]{2,1,0:T(2,128)(2,1)} %reshape.986), calls=%async_computation.3 | async-start | bytes 1572864 | tf_op jit(solution)/shard_map/all_to_all | solution.py:202
  154.3 47.7 %copy-start.72 = (f32[768]{0:T(1024)}, f32[768]{0:T(1024)S(1)}, u32[]{:S(2)}) copy-start(f32[768]{0:T(1024)S(1)} %convert_element_type.270) | copy-start | bytes 9220
  155.0 47.0 %copy-start.84 = (f32[768]{0:T(1024)}, f32[768]{0:T(1024)S(1)}, u32[]{:S(2)}) copy-start(f32[768]{0:T(1024)S(1)} %convert_element_type.274) | copy-start | bytes 9220
  175.7 8.2 slice-start.3
  177.2 6.7 slice-start.4
  181.0 21.1 %copy-start.12 = (f32[1,512,768]{2,1,0:T(8,128)}, f32[1,512,768]{2,1,0:T(8,128)S(1)}, u32[]{:S(2)}) copy-start(f32[1,512,768]{2,1,0:T(8,128)S(1)} %get-tuple-element.709) | copy-start | bytes 4718596
  181.0 21.1 %copy-start.74 = (f32[512]{0:T(512)}, f32[512]{0:T(512)S(1)}, u32[]{:S(2)}) copy-start(f32[512]{0:T(512)S(1)} %broadcast_multiply_fusion.3) | copy-start | bytes 6148
  181.3 20.8 %copy-start.78 = (f32[512]{0:T(512)}, f32[512]{0:T(512)S(1)}, u32[]{:S(2)}) copy-start(f32[512]{0:T(512)S(1)} %fusion.137) | copy-start | bytes 6148
  183.9 14.4 %slice-start = ((s8[9437184]{0:T(1024)(128)(4,1)}), s8[4194304]{0:T(1024)(128)(4,1)S(1)}, s32[]{:S(2)}) async-start(s8[9437184]{0:T(1024)(128)(4,1)} %bitcast.436), calls=%async_computation.19 | async-start | bytes 8388608
  186.6 15.5 %copy-start.28 = (f32[512,3072]{1,0:T(8,128)}, f32[512,3072]{1,0:T(8,128)S(1)}, u32[]{:S(2)}) copy-start(f32[512,3072]{1,0:T(8,128)S(1)} %fusion.152) | copy-start | bytes 18874372
  186.6 11.8 %slice-start.1 = ((s8[9437184]{0:T(1024)(128)(4,1)}), s8[4194304]{0:T(1024)(128)(4,1)S(1)}, s32[]{:S(2)}) async-start(s8[9437184]{0:T(1024)(128)(4,1)} %bitcast.436), calls=%async_computation.20 | async-start | bytes 8388608
  186.6 11.8 %slice-start.2 = ((s8[9437184]{0:T(1024)(128)(4,1)}), s8[1048576]{0:T(1024)(128)(4,1)S(1)}, s32[]{:S(2)}) async-start(s8[9437184]{0:T(1024)(128)(4,1)} %bitcast.436), calls=%async_computation.21 | async-start | bytes 2097152
  202.0 8.6 copy-start.29
  202.1 8.6 copy-start.19
  215.8 13.3 %copy-start.21 = (f32[2048,3]{1,0:T(8,128)S(1)}, f32[2048,3]{1,0:T(8,128)}, u32[]{:S(2)}) copy-start(f32[2048,3]{1,0:T(8,128)} %get-tuple-element.285) | copy-start | bytes 73732
  230.5 5.9 copy-start.15
  253.1 5.6 copy-start.2
  276.5 5.6 copy-start.2
  367.9 28.5 %all-to-all-start.6 = ((bf16[4,2,49152]{2,1,0:T(2,128)(2,1)}), bf16[4,2,49152]{2,1,0:T(2,128)(2,1)}, u32[]{:S(2)}, u32[]{:S(2)}) async-start(bf16[4,2,49152]{2,1,0:T(2,128)(2,1)} %reshape.990), calls=%async_computation.6 | async-start | bytes 1572864 | tf_op jit(solution)/shard_map/all_to_all | solution.py:264
  392.4 8.5 copy-start.27
  396.4 33.0 %all-to-all-start.5 = ((bf16[4,2,49152]{2,1,0:T(2,128)(2,1)}), bf16[4,2,49152]{2,1,0:T(2,128)(2,1)}, u32[]{:S(2)}, u32[]{:S(2)}) async-start(bf16[4,2,49152]{2,1,0:T(2,128)(2,1)} %reshape.992), calls=%async_computation.5 | async-start | bytes 1572864 | tf_op jit(solution)/shard_map/all_to_all | solution.py:263
  400.6 105.5 %reduce-scatter.10.cloned.1.call-start = ((), (), s32[]{:S(2)}) async-start(), calls=%async_computation.15 | async-start | bytes 2654208 | tf_op jit(solution)/shard_map/reduce_scatter | solution.py:313
  429.3 20.0 %all-to-all-start.7 = ((bf16[4,2,49152]{2,1,0:T(2,128)(2,1)}), bf16[4,2,49152]{2,1,0:T(2,128)(2,1)S(1)}, u32[]{:S(2)}, u32[]{:S(2)}) async-start(bf16[4,2,49152]{2,1,0:T(2,128)(2,1)} %reshape.988), calls=%async_computation.7 | async-start | bytes 1572864 | tf_op jit(solution)/shard_map/all_to_all | solution.py:265
  433.5 86.1 %reduce-scatter.6.cloned.1.call-start = ((), (), s32[]{:S(2)}) async-start(), calls=%async_computation.13 | async-start | bytes 2654208 | tf_op jit(solution)/shard_map/reduce_scatter | solution.py:311
  481.3 117.1 %reduce-scatter.8.cloned.1.call-start = ((), (), s32[]{:S(2)}) async-start(), calls=%async_computation.14 | async-start | bytes 7962624 | tf_op jit(solution)/shard_map/reduce_scatter | solution.py:312
  486.3 212.1 %reduce-scatter.14.cloned.1.call-start = ((), (), s32[]{:S(2)}) async-start(), calls=%async_computation.17 | async-start | bytes 10616832 | tf_op jit(solution)/shard_map/reduce_scatter | solution.py:315
  497.9 300.6 %reduce-scatter.12.cloned.1.call-start = ((), (), s32[]{:S(2)}) async-start(), calls=%async_computation.16 | async-start | bytes 10616832 | tf_op jit(solution)/shard_map/reduce_scatter | solution.py:314
  506.0 292.5 %copy-start.95 = (u32[32]{0:T(128)S(1)}, u32[32]{0:T(128)}, u32[]{:S(2)}) copy-start(u32[32]{0:T(128)} %constant.187) | copy-start | bytes 388
  506.0 295.0 %copy-start.65 = (f32[4608]{0:T(1024)S(1)}, f32[4608]{0:T(1024)}, u32[]{:S(2)}) copy-start(f32[4608]{0:T(1024)} %get-tuple-element.747) | copy-start | bytes 55300
  506.0 295.0 %copy-start.86 = (f32[768]{0:T(1024)S(1)}, f32[768]{0:T(1024)}, u32[]{:S(2)}) copy-start(f32[768]{0:T(1024)} %get-tuple-element.700) | copy-start | bytes 9220
  506.0 295.0 %copy-start.89 = (f32[3072]{0:T(1024)S(1)}, f32[3072]{0:T(1024)}, u32[]{:S(2)}) copy-start(f32[3072]{0:T(1024)} %get-tuple-element.702) | copy-start | bytes 36868
  506.0 295.0 %copy-start.91 = (f32[768]{0:T(1024)S(1)}, f32[768]{0:T(1024)}, u32[]{:S(2)}) copy-start(f32[768]{0:T(1024)} %get-tuple-element.620) | copy-start | bytes 9220
  506.1 321.8 %copy-start.36 = (bf16[128,4608]{1,0:T(8,128)(2,1)S(1)}, bf16[128,4608]{1,0:T(8,128)(2,1)}, u32[]{:S(2)}) copy-start(bf16[128,4608]{1,0:T(8,128)(2,1)} %param.29) | copy-start | bytes 3538948
  506.1 321.8 %copy-start.61 = (f32[2,4608]{1,0:T(2,128)S(1)}, f32[2,4608]{1,0:T(2,128)}, u32[]{:S(2)}) copy-start(f32[2,4608]{1,0:T(2,128)} %copy-done.60) | copy-start | bytes 110596
  506.1 393.9 %all-reduce.14.cloned.1.call-start = ((), (), s32[]{:S(2)}) async-start(), calls=%async_computation.18 | async-start | bytes 7667712 | tf_op jit(solution)/shard_map/psum | solution.py:334
  (55 other events, 128.8 us)
Sparse Core Ops, SparseCore 0:
  404.4 38.1 reduce-scatter.9
  481.4 38.1 reduce-scatter.5
  521.9 76.3 reduce-scatter.7
  600.5 97.8 reduce-scatter.13
  700.5 97.8 reduce-scatter.11
  802.0 97.9 all-reduce.13
where the time goes:
time: 925 us; the launch traced here: 914 us
  waiting for transfers between devices  363 us (39%)
  matrix products  176 us (19%)
  local copies, waits for them, and re-layouts  160 us (17%)
  other arithmetic  108 us (12%)
  blocking collectives  61.7 us (7%)
  starting transfers between devices  26.5 us (3%)
  between operations  18.2 us (2%)
    reduce_scatter x1, waiting for transfers between devices, body(): lax.psum_scatter(sum_w_down, 'wide', scatter_dimension=0, tiled=True)  100 us
    reduce_scatter x1, waiting for transfers between devices, body(): lax.psum_scatter(sum_w_up, 'wide', scatter_dimension=0, tiled=True)  100 us
    reduce_scatter x1, waiting for transfers between devices, body(): lax.psum_scatter(sum_w_qkv, 'wide', scatter_dimension=0, tiled=True)  78.7 us
    psum x1, waiting for transfers between devices, body(): lax.psum((share_ada, share_qkv, share_out, share_up, share_down, piece_ad...  60.2 us
    unnamed x190, local copies, waits for them, and re-layouts  58.1 us
    unnamed x8, other arithmetic  53.8 us
    unnamed x1, blocking collectives  26.4 us
    dot_general x4, matrix products, step(): jnp.einsum('shqk,kshd->qshd', grad_scores, keys_doc, preferred_element_ty...  22.6 us
  transfers between devices with their start and end apart: 12, of which 8 were waited for; matrix products, arithmetic and copies ran while one was open for 15% of the time, Pallas kernels for 0%

commit v1 on v0

--- a/solution.py
+++ b/solution.py
@@ -199,13 +199,16 @@
     key_h = head_view(key_h)
     value_h = head_view(value_h)
     mixed_h, logsum = lax.map(attend_row, (query_h, key_h, value_h, docs_per_row))
-    mixed = lax.all_to_all(
-        mixed_h.reshape(count_rows, length, 1, group * head_dim),
-        "narrow",
-        split_axis=1,
-        concat_axis=2,
-        tiled=True,
-    )
+    value = mixed_h.reshape(count_rows, length, 1, group * head_dim)
+    ways, here = (lax.axis_size("narrow"), lax.axis_index("narrow"))
+    width_2 = value.shape[1] // ways
+    turned_2 = jnp.roll(value, -here * width_2, axis=1)
+    got = [lax.slice_in_dim(turned_2, 0, width_2, axis=1)]
+    for far in range(1, ways):
+        sent = lax.slice_in_dim(turned_2, far * width_2, (far + 1) * width_2, axis=1)
+        got.append(lax.ppermute(sent, "narrow", [(d, (d + far) % ways) for d in range(ways)]))
+    line = jnp.concatenate(got[::-1], axis=2)
+    mixed = jnp.roll(line, (here + 1) * got[0].shape[2], axis=2)
     attended = mixed.reshape(count_rows * local, width)
     branch = jnp.dot(attended, w_out, preferred_element_type=jnp.float32).reshape(
         count_rows, local, width

time: 925 us -> 893 us (0.965)
  other arithmetic: 108 us -> 92.4 us
  local copies, waits for them, and re-layouts: 160 us -> 147 us
    unnamed x8 -> x5, other arithmetic: 53.8 us -> 40.2 us
    all_to_all x3 -> x0, local copies, waits for them, and re-layouts: 10.2 us -> none  [body(): lax.all_to_all(mixed_h.reshape(count_rows, length, 1, group * head_dim),...]
    unnamed x190 -> x193, local copies, waits for them, and re-layouts: 58.1 us -> 62.5 us
  transfers between devices with their start and end apart: 12 -> 14, of which waited for: 8 -> 9; matrix products, arithmetic and copies ran while one was open for 15% -> 16% of each run, Pallas kernels for 0% -> 0%
where the time goes in v1:
time: 893 us; the launch traced here: 882 us
  waiting for transfers between devices  361 us (40%)
  matrix products  175 us (20%)
  local copies, waits for them, and re-layouts  147 us (16%)
  other arithmetic  92.4 us (10%)
  blocking collectives  61.6 us (7%)
  starting transfers between devices  25.5 us (3%)
  between operations  18.3 us (2%)
    reduce_scatter x1, waiting for transfers between devices, body(): lax.psum_scatter(sum_w_down, 'wide', scatter_dimension=0, tiled=True)  100 us
    reduce_scatter x1, waiting for transfers between devices, body(): lax.psum_scatter(sum_w_up, 'wide', scatter_dimension=0, tiled=True)  100 us
    reduce_scatter x1, waiting for transfers between devices, body(): lax.psum_scatter(sum_w_qkv, 'wide', scatter_dimension=0, tiled=True)  78.8 us
    unnamed x193, local copies, waits for them, and re-layouts  62.5 us
    psum x1, waiting for transfers between devices, body(): lax.psum((share_ada, share_qkv, share_out, share_up, share_down, piece_ad...  59.6 us
    unnamed x5, other arithmetic  40.2 us
    unnamed x1, blocking collectives  26.4 us
    dot_general x4, matrix products, step(): jnp.einsum('shqk,kshd->qshd', grad_scores, keys_doc, preferred_element_ty...  22.6 us
  transfers between devices with their start and end apart: 14, of which 9 were waited for; matrix products, arithmetic and copies ran while one was open for 16% of the time, Pallas kernels for 0%

profile of v1, /device:TPU:0, one launch (start us, length us, event | category | flops | bytes accessed | tf_op | source)
XLA Modules:
  0.0 882.2 jit_solution(2121860441337367043)
XLA Ops:
  11.4 5.9 copy.302
  22.7 4.2 copy-done.40
  31.4 5.2 all-to-all-start.2
  42.8 4.6 all-to-all-done.2
  47.4 13.2 %all_to_all.87 = bf16[1,512,4,192]{1,3,0,2:T(8,128)(2,1)S(1)} all-to-all(bf16[1,512,4,192]{1,3,0,2:T(8,128)(2,1)S(1)} %get-tuple-element.723), channel_id=1, replica_groups=mesh['narrow'=4,'wide'=8] {'narrow'}, dimensions={2} | all-to-all | bytes 1572864 | tf_op jit(solution)/shard_map/all_to_all | solution.py:193
  77.7 45.2 %conditional.2 = (bf16[2048,3,64]{2,1,0:T(4,128)(2,1)}, f32[2048,3]{1,0:T(8,128)}) conditional(s32[]{:T(128)} %convert_element_type.263, (bf16[2048,3,64]{0,2,1:T(8,128)(2,1)}, bf16[2048,3,64]{0,2,1:T(8,128)(2,1)S(1)}, bf16[2048,3,64]{0,2,1:T(8,128)(2,1)S(1)}) %tuple.47, (bf16[2048,3,64]{0,2,1:T(8,128)(2,1)}, bf16[2048,3,64]{0,2,1:T(8,128)(2,1)S(1)}, ...), branch_computations={%region_2.7_spmd, %region_7.12_spmd} | conditional | flops 833811456 | bytes 64065880 | solution.py:124
  82.1 36.1 %while.50 = (s32[]{:T(128)}, bf16[4,512,1,3,64]{1,4,3,2,0:T(8,128)(2,1)}, f32[4,1,3,512]{3,2,1,0:T(4,128)}, bf16[4,512,1,3,64]{1,4,3,2,0:T(8,128)(2,1)S(1)}, bf1...) while((s32[]{:T(128)}, bf16[4,512,1,3,64]{1,4,3,2,0:T(8,128)(2,1)}, ...), condition=%wide.region_11.11_spmd, body=%wide.region_8.10_spmd.sunk | while | flops 833714688 | bytes 39766112 | solution.py:66
  86.5 4.0 fusion.246
  95.6 4.0 fusion.246
  104.6 4.0 fusion.246
  113.6 4.0 fusion.246
  158.1 11.8 %convert_reduce_fusion = (f32[3072]{0:T(1024)}, bf16[512,3072]{1,0:T(8,128)(2,1)S(1)}) fusion(f32[512,3072]{1,0:T(8,128)S(1)} %fusion.154, f32[3072]{0:T(1024)S(1)} %copy-done.91, bf16[512,768]{1,0:T(8,128)(2,1)S(1)} %copy-done.55, bf16[3072,768]{1,0:T(8,128)(2,1)} %param.37), kind=kOutput, calls=%fused_computation.105 | convolution fusion | flops 2458383360 | bytes 14966784 | tf_op jit(solution)/shard_map/td,fd->tf/dot_general | solution.py:235
  173.6 8.5 fusion.147
  185.3 11.1 %all_to_all.88 = bf16[1,512,4,192]{1,3,0,2:T(8,128)(2,1)S(1)} all-to-all(bf16[1,512,4,192]{1,3,0,2:T(8,128)(2,1)S(1)} %bitcast.474), channel_id=1, replica_groups=mesh['narrow'=4,'wide'=8] {'narrow'}, dimensions={2} | all-to-all | bytes 1572864 | tf_op jit(solution)/shard_map/all_to_all | solution.py:250
  198.5 113.9 %conditional.3 = (bf16[2048,3,64]{2,1,0:T(4,128)(2,1)}, bf16[2048,3,64]{2,1,0:T(4,128)(2,1)}, bf16[2048,3,64]{2,1,0:T(4,128)(2,1)S(1)}) conditional(s32[]{:T(128)} %convert_element_type.263, (bf16[2048,3,64]{0,2,1:T(8,128)(2,1)}, f32[2048,3]{1,0:T(8,128)S(1)}, bf16[2048,3,64]{0,2,1:T(8,128)(2,1)}, bf16[2048,3,64]{0,2,1:T(8,128)(2,1)S(1)}, ...), branch_computations={%region_16.20_spmd, %region_20.24_spmd} | conditional | flops 2053174272 | bytes 155857408 | solution.py:131
  205.1 96.5 %while.53 = (s32[]{:T(128)}, f32[2048,1,3,64]{0,3,2,1:T(8,128)}, f32[2048,1,3,64]{0,3,2,1:T(8,128)}, bf16[4,512,1,3,64]{1,4,3,2,0:T(8,128)(2,1)}, bf16[4,512,1,3...) while((s32[]{:T(128)}, f32[2048,1,3,64]{0,3,2,1:T(8,128)}, ...), condition=%wide.region_23.23_spmd.clone, body=%wide.region_21.22_spmd.clone.sunk | while | flops 2053077504 | bytes 129415344 | solution.py:111
  214.4 4.7 multiply_convert_fusion.8
  219.1 5.6 fusion.232
  229.0 5.1 fusion.231
  237.8 4.7 multiply_convert_fusion.8
  242.5 5.6 fusion.232
  253.9 5.1 fusion.231
  262.6 4.7 multiply_convert_fusion.8
  267.3 5.6 fusion.232
  278.7 5.1 fusion.231
  287.5 4.7 multiply_convert_fusion.8
  292.2 5.6 fusion.232
  301.7 4.2 copy.299
  319.5 12.7 %reduce.19 = bf16[2048,192]{1,0:T(8,128)(2,1)S(1)} reduce(bf16[2048,1,1,192]{3,2,1,0:T(2,128)(2,1)} %bitcast.446, bf16[]{:T(256)} %broadcast.563), dimensions={1,2}, to_apply=%bitcast.289.reduce_sub_computation | reduce | bytes 1572866
  334.6 4.2 all-to-all-start.5
  345.4 13.6 %reduce.18 = bf16[2048,192]{1,0:T(8,128)(2,1)} reduce(bf16[2048,1,1,192]{3,2,1,0:T(2,128)(2,1)} %bitcast.448, bf16[]{:T(256)} %broadcast.563), dimensions={1,2}, to_apply=%bitcast.291.reduce_sub_computation | reduce | bytes 1572866
  359.0 4.0 reshape.989
  363.0 4.2 all-to-all-start.4
  373.6 11.6 %reduce.17 = bf16[2048,192]{1,0:T(8,128)(2,1)S(1)} reduce(bf16[2048,1,1,192]{3,2,1,0:T(2,128)(2,1)S(1)} %bitcast.447, bf16[]{:T(256)} %broadcast.563), dimensions={1,2}, to_apply=%bitcast.287.reduce_sub_computation | reduce | bytes 1572866
  396.0 4.1 all-to-all-start.6
  400.1 4.2 reshape.990
  404.3 4.5 copy.324
  418.6 4.7 copy.332
  450.8 5.0 fusion.121
  456.9 10.4 %fusion.143 = f32[3072,768]{1,0:T(8,128)} fusion(bf16[512,768]{1,0:T(8,128)(2,1)S(1)} %copy-done.56, f32[512,3072]{1,0:T(8,128)} %copy-done.28, f32[3072]{0:T(1024)S(1)} %copy-done.92), kind=kOutput, calls=%fused_computation.236 | convolution fusion | flops 2431647744 | bytes 16527360 | tf_op jit(solution)/shard_map/tf,td->fd/dot_general | solution.py:234
  468.4 7.0 fusion.156
  475.5 12.3 %reduce-scatter.6.cloned.1.call-done = f32[576,128]{1,0:T(8,128)} async-done(((f32[4608,128]{1,0:T(8,128)}), f32[576,128]{1,0:T(8,128)}) %reduce-scatter.6.cloned.1.call-update) | async-done | bytes 294928 | tf_op jit(solution)/shard_map/reduce_scatter | solution.py:314
  487.8 78.8 %reduce-scatter.8.cloned.1.call-done = f32[96,2304]{1,0:T(8,128)} async-done(((f32[768,2304]{1,0:T(8,128)}), f32[96,2304]{1,0:T(8,128)}) %reduce-scatter.8.cloned.1.call-update) | async-done | bytes 884752 | tf_op jit(solution)/shard_map/reduce_scatter | solution.py:315
  566.6 100.1 %reduce-scatter.14.cloned.1.call-done = f32[384,768]{1,0:T(8,128)} async-done(((f32[3072,768]{1,0:T(8,128)}), f32[384,768]{1,0:T(8,128)}) %reduce-scatter.14.cloned.1.call-update) | async-done | bytes 1179664 | tf_op jit(solution)/shard_map/reduce_scatter | solution.py:318
  666.7 100.1 %reduce-scatter.12.cloned.1.call-done = f32[96,3072]{1,0:T(8,128)} async-done(((f32[768,3072]{1,0:T(8,128)}), f32[96,3072]{1,0:T(8,128)}) %reduce-scatter.12.cloned.1.call-update) | async-done | bytes 1179664 | tf_op jit(solution)/shard_map/reduce_scatter | solution.py:317
  769.9 26.4 %all-reduce.9 = (f32[4608]{0:T(1024)S(1)}, f32[768]{0:T(1024)S(1)}, f32[768]{0:T(1024)S(1)}, f32[3072]{0:T(1024)S(1)}, f32[768]{0:T(1024)S(1)}) all-reduce(f32[4608]{0:T(1024)S(1)} %copy-done.69, f32[768]{0:T(1024)S(1)} %get-tuple-element.622, f32[768]{0:T(1024)S(1)} %copy-done.96, ...), channel_id=3, replica_groups=mesh['narrow'=4,'wide'=8] {'wide'}, use_global_device_ids=true, to_apply=%region_30.31.clone | all-reduce | flops 9984 | bytes 79872
  797.7 10.9 %all-reduce.10 = (f32[1,2,128]{2,1,0:T(2,128)}, f32[576]{0:T(1024)}, f32[96]{0:T(128)}, f32[96]{0:T(128)}, f32[384]{0:T(512)}, /*index=5*/f32[96]{0:T(128)}) all-reduce(f32[1,2,128]{2,1,0:T(2,128)S(1)} %convolution_bitcast_fusion.2, f32[576]{0:T(1024)S(1)} %dynamic-slice.2, ...), channel_id=1, replica_groups=mesh['narrow'=4,'wide'=8] {'narrow'}, use_global_device_ids=true, to_apply=%region_26.27 | all-reduce | flops 1504 | bytes 12032 | tf_op jit(solution)/shard_map/psum | solution.py:337
  808.6 59.6 %all-reduce.14.cloned.1.call-done = (f32[128,576]{0,1:T(8,128)}, f32[96,2304]{1,0:T(8,128)}, f32[96,768]{1,0:T(8,128)}, f32[96,3072]{1,0:T(8,128)}, f32[384,768]{1,0:T(8,128)}) async-done(((f32[128,576]{0,1:T(8,128)}, f32[96,2304]{1,0:T(8,128)}, f32[96,768]{1,0:T(8,128)}, f32[96,3072]{1,0:T(8,128)}, f32[384,768]{1,0:T(8,128)}), (f32[128,576]{0,1:T(8,128)}, f32[96,2304]{1,0:T(8,128)}, f32[96,768]{1,0:T(8,128)}, ...) | async-done | bytes 3833872 | tf_op jit(solution)/shard_map/psum | solution.py:337
  (356 shorter events, 243.4 us)
Async XLA Ops:
  7.2 140.8 %copy-start = (bf16[768,768]{1,0:T(8,128)(2,1)S(1)}, bf16[768,768]{1,0:T(8,128)(2,1)}, u32[]{:S(2)}) copy-start(bf16[768,768]{1,0:T(8,128)(2,1)} %param.33) | copy-start | bytes 3538948
  7.2 4.2 copy-start.94
  9.3 12.9 %copy-start.72 = (f32[512]{0:T(512)}, f32[512]{0:T(512)S(1)}, u32[]{:S(2)}) copy-start(f32[512]{0:T(512)S(1)} %broadcast_multiply_fusion.4) | copy-start | bytes 6148
  10.8 11.4 %copy-start.74 = (f32[512]{0:T(512)}, f32[512]{0:T(512)S(1)}, u32[]{:S(2)}) copy-start(f32[512]{0:T(512)S(1)} %fusion.137) | copy-start | bytes 6148
  11.4 10.8 %copy-start.67 = (f32[768]{0:T(1024)}, f32[768]{0:T(1024)S(1)}, u32[]{:S(2)}) copy-start(f32[768]{0:T(1024)S(1)} %convert_element_type.264) | copy-start | bytes 9220
  11.4 5.9 copy-start.35
  11.4 5.9 copy-start.99
  18.3 3.9 copy-start.8
  22.2 6.7 copy-start.6
  22.2 4.7 copy-start.40
  22.7 6.2 copy-start.42
  31.4 16.0 %all-to-all-start.2 = ((bf16[1,512,4,192]{1,3,0,2:T(8,128)(2,1)}), bf16[1,512,4,192]{1,3,0,2:T(8,128)(2,1)S(1)}, u32[]{:S(2)}, u32[]{:S(2)}) async-start(bf16[1,512,4,192]{1,3,0,2:T(8,128)(2,1)} %bitcast.65), calls=%async_computation.2 | async-start | bytes 1572864 | tf_op jit(solution)/shard_map/all_to_all | solution.py:194
  60.6 12.9 %all-to-all-start = ((bf16[1,512,4,192]{1,3,0,2:T(8,128)(2,1)}), bf16[1,512,4,192]{1,3,0,2:T(8,128)(2,1)S(1)}, u32[]{:S(2)}, u32[]{:S(2)}) async-start(bf16[1,512,4,192]{1,3,0,2:T(8,128)(2,1)} %get-tuple-element.724), calls=%async_computation | async-start | bytes 1572864 | tf_op jit(solution)/shard_map/all_to_all | solution.py:192
  126.8 6.1 copy-start.19
  130.0 9.4 %collective-permute-start.1 = (bf16[1,512,1,192]{1,3,2,0:T(8,128)(2,1)}, bf16[1,512,1,192]{1,3,2,0:T(8,128)(2,1)}, u32[]{:S(2)}, u32[]{:S(2)}) collective-permute-start(bf16[1,512,1,192]{1,3,2,0:T(8,128)(2,1)} %get-tuple-element.737), channel_id=1, source_target_pairs={{0,16},{8,24},{16,0},{24,8},{1,17},{9,25},{17,1},{25,9},{2,18},{10... | collective-permute-start | bytes 589832 | tf_op jit(solution)/shard_map/ppermute | solution.py:209
  131.5 4.4 copy-start.98
  131.5 5.1 copy-start.95
  131.5 7.0 collective-permute-start
  135.9 37.6 %copy-start.76 = (f32[768]{0:T(1024)}, f32[768]{0:T(1024)S(1)}, u32[]{:S(2)}) copy-start(f32[768]{0:T(1024)S(1)} %convert_element_type.270) | copy-start | bytes 9220
  136.6 36.9 %copy-start.88 = (f32[768]{0:T(1024)}, f32[768]{0:T(1024)S(1)}, u32[]{:S(2)}) copy-start(f32[768]{0:T(1024)S(1)} %convert_element_type.274) | copy-start | bytes 9220
  137.2 6.8 collective-permute-start.2
  147.9 5.2 copy-start.7
  148.0 3.8 copy-start.26
  151.8 21.7 %copy-start.13 = (f32[1,512,768]{2,1,0:T(8,128)}, f32[1,512,768]{2,1,0:T(8,128)S(1)}, u32[]{:S(2)}) copy-start(f32[1,512,768]{2,1,0:T(8,128)S(1)} %get-tuple-element.709) | copy-start | bytes 4718596
  151.9 21.7 %copy-start.78 = (f32[512]{0:T(512)}, f32[512]{0:T(512)S(1)}, u32[]{:S(2)}) copy-start(f32[512]{0:T(512)S(1)} %broadcast_multiply_fusion.3) | copy-start | bytes 6148
  153.1 20.5 %copy-start.82 = (f32[512]{0:T(512)}, f32[512]{0:T(512)S(1)}, u32[]{:S(2)}) copy-start(f32[512]{0:T(512)S(1)} %fusion.138) | copy-start | bytes 6148
  158.1 15.5 %copy-start.28 = (f32[512,3072]{1,0:T(8,128)}, f32[512,3072]{1,0:T(8,128)S(1)}, u32[]{:S(2)}) copy-start(f32[512,3072]{1,0:T(8,128)S(1)} %fusion.154) | copy-start | bytes 18874372
  173.5 8.6 copy-start.29
  219.1 5.6 copy-start.2
  242.5 5.6 copy-start.2
  267.3 5.6 copy-start.2
  292.2 5.6 copy-start.2
  301.7 4.2 copy-start.5
  334.6 28.5 %all-to-all-start.5 = ((bf16[4,2,49152]{2,1,0:T(2,128)(2,1)}), bf16[4,2,49152]{2,1,0:T(2,128)(2,1)}, u32[]{:S(2)}, u32[]{:S(2)}) async-start(bf16[4,2,49152]{2,1,0:T(2,128)(2,1)} %reshape.987), calls=%async_computation.5 | async-start | bytes 1572864 | tf_op jit(solution)/shard_map/all_to_all | solution.py:267
  359.0 8.4 copy-start.27
  363.0 32.9 %all-to-all-start.4 = ((bf16[4,2,49152]{2,1,0:T(2,128)(2,1)}), bf16[4,2,49152]{2,1,0:T(2,128)(2,1)}, u32[]{:S(2)}, u32[]{:S(2)}) async-start(bf16[4,2,49152]{2,1,0:T(2,128)(2,1)} %reshape.989), calls=%async_computation.4 | async-start | bytes 1572864 | tf_op jit(solution)/shard_map/all_to_all | solution.py:266
  367.2 108.2 %reduce-scatter.10.cloned.1.call-start = ((), (), s32[]{:S(2)}) async-start(), calls=%async_computation.14 | async-start | bytes 2654208 | tf_op jit(solution)/shard_map/reduce_scatter | solution.py:316
  396.0 20.0 %all-to-all-start.6 = ((bf16[4,2,49152]{2,1,0:T(2,128)(2,1)}), bf16[4,2,49152]{2,1,0:T(2,128)(2,1)S(1)}, u32[]{:S(2)}, u32[]{:S(2)}) async-start(bf16[4,2,49152]{2,1,0:T(2,128)(2,1)} %reshape.985), calls=%async_computation.6 | async-start | bytes 1572864 | tf_op jit(solution)/shard_map/all_to_all | solution.py:268
  400.1 87.7 %reduce-scatter.6.cloned.1.call-start = ((), (), s32[]{:S(2)}) async-start(), calls=%async_computation.12 | async-start | bytes 2654208 | tf_op jit(solution)/shard_map/reduce_scatter | solution.py:314
  441.6 4.4 copy-start.100
  449.7 116.9 %reduce-scatter.8.cloned.1.call-start = ((), (), s32[]{:S(2)}) async-start(), calls=%async_computation.13 | async-start | bytes 7962624 | tf_op jit(solution)/shard_map/reduce_scatter | solution.py:315
  455.8 210.9 %reduce-scatter.14.cloned.1.call-start = ((), (), s32[]{:S(2)}) async-start(), calls=%async_computation.16 | async-start | bytes 10616832 | tf_op jit(solution)/shard_map/reduce_scatter | solution.py:318
  467.3 299.4 %reduce-scatter.12.cloned.1.call-start = ((), (), s32[]{:S(2)}) async-start(), calls=%async_computation.15 | async-start | bytes 10616832 | tf_op jit(solution)/shard_map/reduce_scatter | solution.py:317
  475.4 392.8 %all-reduce.14.cloned.1.call-start = ((), (), s32[]{:S(2)}) async-start(), calls=%async_computation.17 | async-start | bytes 7667712 | tf_op jit(solution)/shard_map/psum | solution.py:337
  766.7 30.0 %copy-start.36 = (bf16[128,4608]{1,0:T(8,128)(2,1)S(1)}, bf16[128,4608]{1,0:T(8,128)(2,1)}, u32[]{:S(2)}) copy-start(bf16[128,4608]{1,0:T(8,128)(2,1)} %param.29) | copy-start | bytes 3538948
  766.7 30.0 %copy-start.65 = (f32[2,4608]{1,0:T(2,128)S(1)}, f32[2,4608]{1,0:T(2,128)}, u32[]{:S(2)}) copy-start(f32[2,4608]{1,0:T(2,128)} %copy-done.64) | copy-start | bytes 110596
  868.2 3.9 copy-start.66
  868.2 4.7 copy-start.52
  (57 other events, 103.5 us)
Sparse Core Ops, SparseCore 0:
  371.0 37.9 reduce-scatter.9
  449.8 37.9 reduce-scatter.5
  490.1 76.3 reduce-scatter.7
  568.7 97.8 reduce-scatter.13
  668.8 97.8 reduce-scatter.11
  770.3 97.9 all-reduce.13
